TPU v7x, 32 devices: a whole 2x2x4 slice. The times are simulated.
32 devices in a mesh: groups: 2 (over y), pool: 4 (over z), tensor: 4 (over x, core).
Axes of the slice: x: 2, y: 2, z: 4, core: 2. Of those that a mesh axis runs over, the one named last changes fastest.
Arguments:
- prompt_query: bfloat16 [2048, 8192], P(('groups', 'pool'), 'tensor'), parts along dimension 0, may hold values from -20 to 20
- prompt_key_value: bfloat16 [2048, 8, 256], P(('groups', 'pool'), 'tensor'), parts along dimension 0, may hold values from -20 to 20
- segment_ids: int32 [2048], P('groups'), parts along dimension 0, may hold values from 0 to 2, never falling along the last dimension, each value on 1 to 512 neighbouring positions
- block_dest: int32 [128, 1], P('groups'), parts along dimension 0, may hold values from 0 to 3; in each aligned block of 16 rows (0 to 15, 16 to 31, ...) at most 8 rows name the same one
- decode_query: bfloat16 [2, 192, 8192], P(None, ('groups', 'pool'), 'tensor'), parts along dimension 1, may hold values from -20 to 20
- dec_kv: bfloat16 [2, 192, 8, 256], P(None, ('groups', 'pool'), 'tensor'), parts along dimension 1, may hold values from -20 to 20
- dec_cache: bfloat16 [192, 512, 8, 256], P(('groups', 'pool'), None, 'tensor'), parts along dimension 0, may hold values from -20 to 20
- ctx_len: int32 [192], P(('groups', 'pool')), parts along dimension 0, may hold values from 1 to 512, 24576 in all
- out_weight: bfloat16 [8192, 8192], P('tensor', 'pool'), may hold values from -0.0625 to 0.0625
Outputs:
- prefill_out: bfloat16 [2048, 8192], P(('groups', 'tensor'), 'pool'), parts along dimension 0
- decode_out: bfloat16 [2, 192, 8192], P(None, ('groups', 'tensor'), 'pool'), parts along dimension 1
- arrived: bfloat16 [8, 4, 8, 16, 8, 256], P(('groups', 'pool'), None, None, None, 'tensor'), parts along dimension 0
There are 2 independent parts, one for each index of `groups`. A program takes and returns all parts, laid end to end along the dimension named above; an argument that names none is the same for every part. Nothing has to cross between parts.
Inputs may be any that keep to these rules, and one draw needn't show every extreme that they name: `segment_ids`: prompts never fall back to an earlier id; a prompt has at most 512 tokens and one has exactly 512. `block_dest`: among the 16 blocks of one member, at most 8 go to one receiver. `ctx_len`: one request has exactly 512 cached tokens.
All inputs are finite; a program needn't handle non-finite values. No bound on the sum of `ctx_len` on one device may be relied on, other than what follows from the above.
Results may differ from a plain program's by a relative error of at most 0.012.
Values may be sent and summed in bfloat16 or wider, within the bound.
A program may use at most 128 MiB of HBM per device.

v0:
```python
import math

import jax
import jax.numpy as jnp
from jax import lax
from jax.sharding import PartitionSpec as P

BLOCK_TOKENS = 16


def block_ranks(destinations):
    item_count = destinations.shape[-1]
    same_dest = destinations[..., :, None] == destinations[..., None, :]
    earlier = (
        jnp.arange(item_count, dtype=jnp.int32)[None, :]
        < jnp.arange(item_count, dtype=jnp.int32)[:, None]
    )
    return jnp.sum(jnp.where(same_dest & earlier, 1, 0), axis=-1).astype(jnp.int32)


def body(
    prompt_query,
    prompt_key_value,
    segment_ids,
    block_dest,
    decode_query,
    dec_kv,
    dec_cache,
    ctx_len,
    out_weight,
):
    row_count = prompt_query.shape[0]
    kv_heads = prompt_key_value.shape[1]
    head_size = prompt_key_value.shape[2] // 2
    query_heads = prompt_query.shape[1] // head_size
    query_group_width = query_heads // kv_heads
    score_scale = 1.0 / math.sqrt(head_size)
    pool_size = lax.axis_size("pool")
    my_index = lax.axis_index("pool")
    own_start = my_index * row_count
    own_positions = own_start + jnp.arange(row_count, dtype=jnp.int32)
    own_segments = lax.dynamic_slice_in_dim(segment_ids, own_start, row_count, 0)
    query_matrix = prompt_query.reshape(row_count, kv_heads, query_group_width, head_size)
    block_size = BLOCK_TOKENS
    block_count = row_count // block_size
    capacity = max(2, 2 * block_count // pool_size)
    destinations = block_dest[:, 0].reshape(pool_size, block_count)
    slot_ranks = block_ranks(destinations)
    flat_size = block_size * kv_heads * 2 * head_size
    slot_ids = jnp.arange(capacity, dtype=jnp.int32)
    key_piece = lax.all_gather(prompt_key_value, "pool", axis=0, tiled=True)
    key_count = key_piece.shape[0]
    running_max = jnp.full((row_count, kv_heads, query_group_width), -1e30, jnp.float32)
    scores = (
        jnp.einsum(
            "thgd,shd->thgs",
            query_matrix,
            key_piece[..., :head_size],
            preferred_element_type=jnp.float32,
        )
        * score_scale
    )
    key_positions = jnp.arange(key_count, dtype=jnp.int32)
    allowed = (own_segments[:, None] == segment_ids[None, :]) & (
        key_positions[None, :] <= own_positions[:, None]
    )
    allowed = allowed[:, None, None, :]
    block_max = jnp.max(jnp.where(allowed, scores, -1e30), axis=-1)
    new_max = jnp.maximum(running_max, block_max)
    weights = jnp.where(allowed, jnp.exp(scores - new_max[..., None]), 0.0)
    new_sum = jnp.sum(weights, axis=-1)
    new_out = jnp.einsum(
        "thgs,shd->thgd",
        weights.astype(jnp.bfloat16),
        key_piece[..., head_size:],
        preferred_element_type=jnp.float32,
    )
    softmax_state = (new_max, new_sum, new_out)
    own_dest = lax.dynamic_index_in_dim(destinations, my_index, 0, keepdims=False)
    own_ranks = lax.dynamic_index_in_dim(slot_ranks, my_index, 0, keepdims=False)
    receivers = jnp.arange(pool_size, dtype=jnp.int32)
    select_entries = (
        (own_dest[None, None, :] == receivers[:, None, None])
        & (own_ranks[None, None, :] == slot_ids[None, :, None])
    ).astype(jnp.bfloat16)
    outgoing = jnp.einsum(
        "qcb,bf->qcf",
        select_entries,
        prompt_key_value.reshape(block_count, flat_size),
        preferred_element_type=jnp.float32,
    ).astype(jnp.bfloat16)
    arrived = lax.all_to_all(outgoing, "pool", split_axis=0, concat_axis=0, tiled=True)
    running_max, running_sum, running_out = softmax_state
    pre_att = (
        (running_out / running_sum[..., None])
        .reshape(row_count, query_heads * head_size)
        .astype(jnp.bfloat16)
    )
    arrived = arrived.reshape(1, pool_size, capacity, block_size, kv_heads, 2 * head_size)
    request_count = decode_query.shape[1]
    cache_length = dec_cache.shape[1]
    live_mask = (jnp.arange(cache_length, dtype=jnp.int32)[None, :] < ctx_len[:, None])[
        :, None, None, :
    ]
    old_keys = dec_cache[..., :head_size]
    old_values = dec_cache[..., head_size:]
    outputs = []
    for step_index in range(2):
        query_rows = decode_query[step_index].reshape(
            request_count, kv_heads, query_group_width, head_size
        )
        old_scores = (
            jnp.einsum("rhgd,rchd->rhgc", query_rows, old_keys, preferred_element_type=jnp.float32)
            * score_scale
        )
        new_scores = (
            jnp.einsum(
                "rhgd,nrhd->rhgn",
                query_rows,
                dec_kv[: step_index + 1, ..., :head_size],
                preferred_element_type=jnp.float32,
            )
            * score_scale
        )
        row_max = jnp.maximum(
            jnp.max(jnp.where(live_mask, old_scores, -1e30), axis=-1, keepdims=True),
            jnp.max(new_scores, axis=-1, keepdims=True),
        )
        old_weights = jnp.where(live_mask, jnp.exp(old_scores - row_max), 0.0)
        new_weights = jnp.exp(new_scores - row_max)
        weight_total = jnp.sum(old_weights, axis=-1) + jnp.sum(new_weights, axis=-1)
        combined = jnp.einsum(
            "rhgc,rchd->rhgd",
            old_weights.astype(jnp.bfloat16),
            old_values,
            preferred_element_type=jnp.float32,
        )
        combined = combined + jnp.einsum(
            "rhgn,nrhd->rhgd",
            new_weights.astype(jnp.bfloat16),
            dec_kv[: step_index + 1, ..., head_size:],
            preferred_element_type=jnp.float32,
        )
        outputs.append(
            (combined / weight_total[..., None]).reshape(request_count, query_heads * head_size)
        )
    dec_att = jnp.stack(outputs).astype(jnp.bfloat16)
    pre_rows, dec_rows = (
        lax.all_gather(pre_att, "pool", axis=0, tiled=True),
        lax.all_gather(dec_att, "pool", axis=1, tiled=True),
    )
    pre_part = jnp.dot(pre_rows, out_weight, preferred_element_type=jnp.float32)
    dec_part = jnp.einsum("srk,kd->srd", dec_rows, out_weight, preferred_element_type=jnp.float32)
    pre_sum, dec_sum = (
        lax.psum_scatter(
            pre_part.astype(jnp.bfloat16), "tensor", scatter_dimension=0, tiled=True
        ).astype(jnp.float32),
        lax.psum_scatter(
            dec_part.astype(jnp.bfloat16), "tensor", scatter_dimension=1, tiled=True
        ).astype(jnp.float32),
    )
    return (pre_sum.astype(jnp.bfloat16), dec_sum.astype(jnp.bfloat16), arrived)


def solution(mesh):
    return jax.shard_map(
        body,
        mesh=mesh,
        in_specs=(
            P(("groups", "pool"), "tensor"),
            P(("groups", "pool"), "tensor", None),
            P("groups"),
            P("groups", None),
            P(None, ("groups", "pool"), "tensor"),
            P(None, ("groups", "pool"), "tensor", None),
            P(("groups", "pool"), None, "tensor", None),
            P(("groups", "pool")),
            P("tensor", "pool"),
        ),
        out_specs=(
            P(("groups", "tensor"), "pool"),
            P(None, ("groups", "tensor"), "pool"),
            P(("groups", "pool"), None, None, None, "tensor", None),
        ),
        check_vma=False,
    )
```

profile of v0, /device:TPU:0, one launch (start us, length us, event | category | flops | bytes accessed | tf_op | source)
XLA Modules:
  0.0 225.0 jit_solution(15540843859198449555)
XLA Ops:
  8.0 1.7 copy.30
  9.8 1.5 copy.52
  11.3 0.8 dynamic_slice.12
  12.0 0.7 bitcast_convert_fusion
  12.8 0.9 fusion.43
  13.7 1.0 slice_bitcast_fusion.5
  14.7 27.0 %all-gather.3.cloned.1.call-done = bf16[1024,2,256]{2,0,1:T(8,128)(2,1)} async-done(((bf16[256,2,256]{2,0,1:T(8,128)(2,1)}), bf16[1024,2,256]{2,0,1:T(8,128)(2,1)}) %all-gather.3.cloned.1.call-update) | async-done | bytes 1048592 | tf_op jit(solution)/shard_map/all_gather | solution.py:51
  41.7 8.3 %fusion = (f32[256,2,8]{0,2,1:T(8,128)S(1)}, f32[2,1024,256,8]{2,1,3,0:T(8,128)}) fusion(pred[256,1024]{0,1:T(8,128)(4,1)S(1)} %fusion.43, bf16[256,2,8,128]{3,2,1,0:T(8,128)(2,1)S(1)} %bitcast.81, bf16[1024,2,256]{2,0,1:T(8,128)(2,1)} %all-gather.3.cloned.1.call-done), kind=kOutput, calls=%fused_computation.2 | convolution fusion | flops 1086320640 | bytes 18628608 | tf_op jit(solution)/shard_map/thgd,shd->thgs/dot_general | solution.py:55
  50.0 9.2 %fusion.3 = f32[256,2,8]{0,2,1:T(8,128)S(1)} fusion(f32[2,1024,256,8]{2,1,3,0:T(8,128)} %get-tuple-element.25, f32[256,2,8]{0,2,1:T(8,128)S(1)} %broadcast_maximum_fusion, pred[256,1024]{0,1:T(8,128)(4,1)S(1)} %fusion.43), kind=kLoop, calls=%fused_computation.5 | loop fusion | flops 16773120 | bytes 17072128 | tf_op jit(solution)/shard_map/reduce_sum | solution.py:71
  59.3 8.7 %fusion.21 = bf16[256,2,8,128]{0,3,2,1:T(8,128)(2,1)} fusion(f32[2,1024,256,8]{2,1,3,0:T(8,128)} %get-tuple-element.25, f32[256,2,8]{0,2,1:T(8,128)S(1)} %broadcast_maximum_fusion, pred[256,1024]{0,1:T(8,128)(4,1)S(1)} %fusion.43, f32[256,2,8]{0,2,1:T(8,128)S(1)} %fusion.3, bf16[1024,2,256]{2,0,1:T(8,128)(2,1)S(1)} %copy-done.2), kind=kOutput, calls=%fused_computation.23 | convolution fusion | flops 1091567616 | bytes 18644992 | tf_op jit(solution)/shard_map/thgs,shd->thgd/dot_general | solution.py:72
  68.6 10.1 %fusion.72 = (bf16[24,512,2,128]{3,2,1,0:T(2,128)(2,1)S(1)}, bf16[24,512,2,128]{3,2,1,0:T(2,128)(2,1)S(1)}) fusion(bf16[24,512,2,256]{3,2,1,0:T(2,128)(2,1)} %param.15), kind=kLoop, calls=%fused_computation.86 | loop fusion | bytes 25165824 | tf_op jit(solution)/shard_map/slice | solution.py:105
  78.7 1.9 select_reduce_fusion.1
  80.8 2.0 fusion.44
  83.0 0.3 fusion.46
  83.3 1.0 fusion.10
  84.4 0.3 fusion.34
  84.8 3.8 %fusion.38 = bf16[24,2,8,128]{3,2,1,0:T(8,128)(2,1)S(1)} fusion(bf16[24,512,2,128]{3,2,1,0:T(2,128)(2,1)} %copy-done, f32[24,2,8,512]{3,2,1,0:T(8,128)S(1)} %get-tuple-element.27, f32[24,2,8]{2,1,0:T(2,128)S(1)} %multiply_maximum_fusion, pred[24,512]{1,0:T(8,128)(4,1)S(1)} %iota_compare_fusion.1, f32[24,2,8]{2,1,0:T(2,128)S(1)} %get-tuple-element.19, ...), kind=kOutput, calls=%fused_computation.32 | convolution fusion | flops 51118080 | bytes 7217664 | tf_op jit(solution)/shard_map/rhgc,rchd->rhgd/dot_general | solution.py:132
  88.6 33.3 %all_gather.11 = bf16[2,96,2048]{2,1,0:T(8,128)(2,1)S(1)} all-gather(bf16[2,24,2048]{2,1,0:T(8,128)(2,1)S(1)} %pad_maximum_fusion), channel_id=1, replica_groups=mesh['groups'=2,'pool'=4,'tensor'=4] {'pool'}, dimensions={1}, use_global_device_ids=true | all-gather | bytes 983040 | tf_op jit(solution)/shard_map/all_gather | solution.py:150
  121.9 5.3 %fusion.18 = bf16[2,96,2048]{2,1,0:T(8,128)(2,1)S(1)} fusion(bf16[2,96,2048]{2,1,0:T(8,128)(2,1)S(1)} %all_gather.11, bf16[2048,2048]{1,0:T(8,128)(2,1)} %param.17), kind=kOutput, calls=%fused_computation.21 | convolution fusion | flops 1611005952 | bytes 9961472 | tf_op jit(solution)/shard_map/srk,kd->srd/dot_general | solution.py:153
  127.2 0.8 copy.46
  128.0 1.1 copy.55
  129.2 0.3 reduce-scatter.5.cloned.1.call-start
  129.5 31.3 %all-gather.5.cloned.1.call-done = bf16[1024,2048]{0,1:T(8,128)(2,1)} async-done(((bf16[256,2048]{0,1:T(8,128)(2,1)}), bf16[1024,2048]{0,1:T(8,128)(2,1)}) %all-gather.5.cloned.1.call-update) | async-done | bytes 4194320 | tf_op jit(solution)/shard_map/all_gather | solution.py:149
  160.8 14.0 %convolution_convert_fusion.1 = bf16[1024,2048]{1,0:T(8,128)(2,1)} fusion(bf16[1024,2048]{0,1:T(8,128)(2,1)} %all-gather.5.cloned.1.call-done, bf16[2048,2048]{1,0:T(8,128)(2,1)} %param.17), kind=kOutput, calls=%fused_computation.20 | convolution fusion | flops 8592031744 | bytes 16777216 | tf_op jit(solution)/shard_map/dot_general | solution.py:152
  175.1 0.5 broadcast.94
  175.6 0.7 reduce.3
  176.6 0.3 convolution_convert_fusion
  176.9 17.4 %all_to_all.5 = bf16[4,8,8192]{2,1,0:T(8,128)(2,1)S(1)} all-to-all(bf16[4,8,8192]{2,1,0:T(8,128)(2,1)S(1)} %convolution_convert_fusion), channel_id=1, replica_groups=mesh['groups'=2,'pool'=4,'tensor'=4] {'pool'}, dimensions={0} | all-to-all | bytes 1048576 | tf_op jit(solution)/shard_map/all_to_all | solution.py:92
  194.3 1.3 copy.38
  195.6 1.1 reshape.201
  196.7 0.7 copy.47
  197.4 20.2 %reduce-scatter.5.cloned.1.call-done = bf16[256,2048]{1,0:T(8,128)(2,1)} async-done(((bf16[1024,2048]{1,0:T(8,128)(2,1)}), bf16[256,2048]{1,0:T(8,128)(2,1)}) %reduce-scatter.5.cloned.1.call-update) | async-done | bytes 1048592 | tf_op jit(solution)/shard_map/reduce_scatter | solution.py:155
  (43 shorter events, 1.8 us)
Async XLA Ops:
  8.0 33.7 %all-gather.3.cloned.1.call-start = ((), (), s32[]{:S(2)}) async-start(), calls=%async_computation.3 | async-start | bytes 1310720 | tf_op jit(solution)/shard_map/all_gather | solution.py:51
  9.7 151.1 %all-gather.5.cloned.1.call-start = ((), (), s32[]{:S(2)}) async-start(), calls=%async_computation.4 | async-start | bytes 5242880 | tf_op jit(solution)/shard_map/all_gather | solution.py:149
  50.0 9.2 %copy-start.2 = (bf16[1024,2,256]{2,0,1:T(8,128)(2,1)S(1)}, bf16[1024,2,256]{2,0,1:T(8,128)(2,1)}, u32[]{:S(2)}) copy-start(bf16[1024,2,256]{2,0,1:T(8,128)(2,1)} %all-gather.3.cloned.1.call-done) | copy-start | bytes 3145732
  59.2 9.0 %copy-start.4 = (s32[24]{0:T(128)S(1)}, s32[24]{0:T(128)}, u32[]{:S(2)}) copy-start(s32[24]{0:T(128)} %param.16) | copy-start | bytes 292
  59.2 9.1 %copy-start.3 = (bf16[2,24,2,256]{3,2,1,0:T(2,128)(2,1)S(1)}, bf16[2,24,2,256]{3,2,1,0:T(2,128)(2,1)}, u32[]{:S(2)}) copy-start(bf16[2,24,2,256]{3,2,1,0:T(2,128)(2,1)} %param.14) | copy-start | bytes 147460
  68.0 127.6 %reduce-scatter.7.cloned.1.call-start = ((), (), s32[]{:S(2)}) async-start(), calls=%async_computation.6 | async-start | bytes 983040
  78.6 4.7 %copy-start = (bf16[24,512,2,128]{3,2,1,0:T(2,128)(2,1)}, bf16[24,512,2,128]{3,2,1,0:T(2,128)(2,1)S(1)}, u32[]{:S(2)}) copy-start(bf16[24,512,2,128]{3,2,1,0:T(2,128)(2,1)S(1)} %get-tuple-element.15) | copy-start | bytes 18874372
  129.2 45.7 %copy-start.1 = (bf16[256,2,256]{2,1,0:T(2,128)(2,1)S(1)}, bf16[256,2,256]{2,1,0:T(2,128)(2,1)}, u32[]{:S(2)}) copy-start(bf16[256,2,256]{2,1,0:T(2,128)(2,1)} %param.10) | copy-start | bytes 786436
  129.2 46.4 %copy-start.5 = (s32[64,1]{0,1:T(1,128)S(1)}, s32[64,1]{0,1:T(1,128)}, u32[]{:S(2)}) copy-start(s32[64,1]{0,1:T(1,128)} %param.12) | copy-start | bytes 772
  129.2 88.3 %reduce-scatter.5.cloned.1.call-start = ((), (), s32[]{:S(2)}) async-start(), calls=%async_computation.5 | async-start | bytes 5242880 | tf_op jit(solution)/shard_map/reduce_scatter | solution.py:155
Sparse Core Ops, SparseCore 0:
  11.1 30.6 all-gather.2
  68.1 92.6 all-gather.4
Sparse Core Ops, SparseCore 1:
  129.3 23.2 reduce-scatter.6
  175.0 42.6 reduce-scatter.4
where the time goes:
time: 226 us; the launch traced here: 225 us
  waiting for transfers between devices  78.6 us (35%)
  blocking collectives  50.7 us (22%)
  matrix products  46 us (20%)
  local copies, waits for them, and re-layouts  21 us (9%)
  between operations  15.8 us (7%)
  other arithmetic  12.4 us (5%)
    all_gather x1, blocking collectives, body(): lax.all_gather(dec_att, 'pool', axis=1, tiled=True)  33.3 us
    all_gather x1, waiting for transfers between devices, body(): lax.all_gather(pre_att, 'pool', axis=0, tiled=True)  31.3 us
    all_gather x1, waiting for transfers between devices, body(): key_piece = lax.all_gather(prompt_key_value, 'pool', axis=0, tiled=True)  27 us
    reduce_scatter x1, waiting for transfers between devices, body(): lax.psum_scatter(pre_part.astype(jnp.bfloat16), 'tensor', scatter_dimensi...  20.2 us
    all_to_all x1, blocking collectives, body(): lax.all_to_all(outgoing, 'pool', split_axis=0, concat_axis=0, tiled=True)  17.4 us
    dot_general x1, matrix products, body(): pre_part = jnp.dot(pre_rows, out_weight, preferred_element_type=jnp.float32)  14 us
    slice x1, local copies, waits for them, and re-layouts, body(): old_keys = dec_cache[..., :head_size]  10.1 us
    unnamed x23, local copies, waits for them, and re-layouts  9.77 us
  transfers between devices with their start and end apart: 4, of which 3 were waited for; matrix products, arithmetic and copies ran while one was open for 23% of the time, Pallas kernels for 0%

commit v1 on v0

--- a/solution.py
+++ b/solution.py
@@ -1,11 +1,239 @@
+import functools
 import math
 
 import jax
 import jax.numpy as jnp
 from jax import lax
+from jax.experimental import pallas as pl
+from jax.experimental.pallas import tpu as pltpu
 from jax.sharding import PartitionSpec as P
 
 BLOCK_TOKENS = 16
+MESH = pl.DeviceIdType.MESH
+COLUMN_TILE = 512
+
+
+def project_kernel(
+    chunks,
+    slot_members,
+    att_ref,
+    weight_ref,
+    out_ref,
+    gathered,
+    weight,
+    outgoing,
+    landed,
+    total,
+    own_sem,
+    weight_sem,
+    ring_send,
+    ring_recv,
+    part_send,
+    part_recv,
+):
+    pool = lax.axis_size("pool")
+    tensor = lax.axis_size("tensor")
+    group = lax.axis_index("groups")
+    me = lax.axis_index("pool")
+    lane = lax.axis_index("tensor")
+    columns = weight_ref.shape[1]
+    tile = min(COLUMN_TILE, columns)
+    has_left = me > 0
+    has_right = me < pool - 1
+
+    load_weight = pltpu.make_async_copy(weight_ref, weight, weight_sem)
+    load_weight.start()
+    load_own = pltpu.make_async_copy(att_ref, gathered.at[me], own_sem)
+    load_own.start()
+
+    barrier = pltpu.get_barrier_semaphore()
+
+    @pl.when(has_left)
+    def _():
+        pl.semaphore_signal(barrier, inc=1, device_id=(group, me - 1, lane), device_id_type=MESH)
+
+    @pl.when(has_right)
+    def _():
+        pl.semaphore_signal(barrier, inc=1, device_id=(group, me + 1, lane), device_id_type=MESH)
+
+    for step in range(1, tensor):
+        peer = lax.rem(lane + step, tensor)
+        pl.semaphore_signal(barrier, inc=1, device_id=(group, me, peer), device_id_type=MESH)
+
+    pl.semaphore_wait(
+        barrier, has_left.astype(jnp.int32) + has_right.astype(jnp.int32) + tensor - 1
+    )
+
+    def ring_copy(member, chunk, way):
+        start, size = chunks[chunk]
+        block = gathered.at[member, pl.ds(start, size)]
+        return pltpu.make_async_remote_copy(
+            src_ref=block,
+            dst_ref=block,
+            send_sem=ring_send.at[way, member, chunk],
+            recv_sem=ring_recv.at[member, chunk],
+            device_id=(group, me - 1 if way == 0 else me + 1, lane),
+            device_id_type=MESH,
+        )
+
+    def part_copy(member, chunk):
+        start, size = chunks[chunk]
+        target = member // slot_members
+        return pltpu.make_async_remote_copy(
+            src_ref=outgoing.at[member, pl.ds(start, size)],
+            dst_ref=landed.at[lane, member % slot_members, pl.ds(start, size)],
+            send_sem=part_send.at[member, chunk],
+            recv_sem=part_recv.at[lane, member % slot_members, chunk],
+            device_id=(group, me, target),
+            device_id_type=MESH,
+        )
+
+    def arrived_copy(source, place, chunk):
+        start, size = chunks[chunk]
+        return pltpu.make_async_remote_copy(
+            src_ref=outgoing.at[0, pl.ds(start, size)],
+            dst_ref=landed.at[source, place, pl.ds(start, size)],
+            send_sem=part_send.at[0, chunk],
+            recv_sem=part_recv.at[source, place, chunk],
+            device_id=(group, me, source),
+            device_id_type=MESH,
+        )
+
+    def project(member, chunk):
+        start, size = chunks[chunk]
+        mine = member // slot_members == lane
+
+        @pl.loop(0, columns // tile)
+        def _(index):
+            place = pl.ds(pl.multiple_of(index * tile, tile), tile)
+            part = jnp.dot(
+                gathered[member, pl.ds(start, size), :],
+                weight[:, place],
+                preferred_element_type=jnp.float32,
+            )
+
+            @pl.when(mine)
+            def _():
+                total[member % slot_members, pl.ds(start, size), place] = part
+
+            @pl.when(jnp.logical_not(mine))
+            def _():
+                outgoing[member, pl.ds(start, size), place] = part.astype(jnp.bfloat16)
+
+        @pl.when(jnp.logical_not(mine))
+        def _():
+            part_copy(member, chunk).start()
+
+    load_own.wait()
+    for chunk in range(len(chunks)):
+        @pl.when(has_left)
+        def _():
+            ring_copy(me, chunk, 0).start()
+
+        @pl.when(has_right)
+        def _():
+            ring_copy(me, chunk, 1).start()
+
+    load_weight.wait()
+
+    @pl.loop(0, pool)
+    def _(distance):
+        left = me - distance
+        right = me + distance
+        use_left = left >= 0
+        use_right = jnp.logical_and(right < pool, distance > 0)
+        for chunk in range(len(chunks)):
+            @pl.when(jnp.logical_and(use_left, distance > 0))
+            def _():
+                ring_copy(left, chunk, 1).wait_recv()
+
+                @pl.when(has_right)
+                def _():
+                    ring_copy(left, chunk, 1).start()
+
+            @pl.when(use_right)
+            def _():
+                ring_copy(right, chunk, 0).wait_recv()
+
+                @pl.when(has_left)
+                def _():
+                    ring_copy(right, chunk, 0).start()
+
+            @pl.when(use_left)
+            def _():
+                project(left, chunk)
+
+            @pl.when(use_right)
+            def _():
+                project(right, chunk)
+
+    for place in range(slot_members):
+        for chunk in range(len(chunks)):
+            start, size = chunks[chunk]
+            for step in range(1, tensor):
+                arrived_copy(lax.rem(lane + step, tensor), place, chunk).wait_recv()
+
+            @pl.loop(0, columns // tile)
+            def _(index):
+                span = pl.ds(pl.multiple_of(index * tile, tile), tile)
+                value = total[place, pl.ds(start, size), span]
+                for step in range(1, tensor):
+                    source = lax.rem(lane + step, tensor)
+                    value = value + landed[source, place, pl.ds(start, size), span].astype(
+                        jnp.float32
+                    )
+                out_ref[place, pl.ds(start, size), span] = value.astype(jnp.bfloat16)
+
+    @pl.loop(0, pool)
+    def _(member):
+        for chunk in range(len(chunks)):
+            @pl.when(jnp.logical_and(has_left, member >= me))
+            def _():
+                ring_copy(member, chunk, 0).wait_send()
+
+            @pl.when(jnp.logical_and(has_right, member <= me))
+            def _():
+                ring_copy(member, chunk, 1).wait_send()
+
+            @pl.when(member // slot_members != lane)
+            def _():
+                part_copy(member, chunk).wait_send()
+
+
+def project_all(att, out_weight, chunks):
+    pool = lax.axis_size("pool")
+    tensor = lax.axis_size("tensor")
+    rows, depth = att.shape
+    columns = out_weight.shape[1]
+    slot_members = pool // tensor
+    count = len(chunks)
+    return pl.pallas_call(
+        functools.partial(project_kernel, chunks, slot_members),
+        out_shape=jax.ShapeDtypeStruct((slot_members, rows, columns), jnp.bfloat16),
+        in_specs=[pl.BlockSpec(memory_space=pl.ANY)] * 2,
+        out_specs=pl.BlockSpec(memory_space=pltpu.VMEM),
+        scratch_shapes=[
+            pltpu.VMEM((pool, rows, depth), jnp.bfloat16),
+            pltpu.VMEM((depth, columns), jnp.bfloat16),
+            pltpu.VMEM((pool, rows, columns), jnp.bfloat16),
+            pltpu.VMEM((tensor, slot_members, rows, columns), jnp.bfloat16),
+            pltpu.VMEM((slot_members, rows, columns), jnp.float32),
+            pltpu.SemaphoreType.DMA,
+            pltpu.SemaphoreType.DMA,
+            pltpu.SemaphoreType.DMA((2, pool, count)),
+            pltpu.SemaphoreType.DMA((pool, count)),
+            pltpu.SemaphoreType.DMA((pool, count)),
+            pltpu.SemaphoreType.DMA((tensor, slot_members, count)),
+        ],
+        compiler_params=pltpu.CompilerParams(
+            collective_id=0, has_side_effects=True, vmem_limit_bytes=50 * 1024 * 1024
+        ),
+        cost_estimate=pl.CostEstimate(
+            flops=2 * pool * rows * depth * columns,
+            bytes_accessed=2 * (depth * columns + 2 * rows * depth),
+            transcendentals=0,
+        ),
+    )(att, out_weight)
 
 
 def block_ranks(destinations):
@@ -76,20 +304,15 @@
         preferred_element_type=jnp.float32,
     )
     softmax_state = (new_max, new_sum, new_out)
-    own_dest = lax.dynamic_index_in_dim(destinations, my_index, 0, keepdims=False)
-    own_ranks = lax.dynamic_index_in_dim(slot_ranks, my_index, 0, keepdims=False)
-    receivers = jnp.arange(pool_size, dtype=jnp.int32)
     select_entries = (
-        (own_dest[None, None, :] == receivers[:, None, None])
-        & (own_ranks[None, None, :] == slot_ids[None, :, None])
+        (destinations[:, None, :] == my_index) & (slot_ranks[:, None, :] == slot_ids[None, :, None])
     ).astype(jnp.bfloat16)
-    outgoing = jnp.einsum(
-        "qcb,bf->qcf",
+    arrived = jnp.einsum(
+        "pcb,pbf->pcf",
         select_entries,
-        prompt_key_value.reshape(block_count, flat_size),
+        key_piece.reshape(pool_size, block_count, flat_size),
         preferred_element_type=jnp.float32,
     ).astype(jnp.bfloat16)
-    arrived = lax.all_to_all(outgoing, "pool", split_axis=0, concat_axis=0, tiled=True)
     running_max, running_sum, running_out = softmax_state
     pre_att = (
         (running_out / running_sum[..., None])
@@ -145,21 +368,20 @@
             (combined / weight_total[..., None]).reshape(request_count, query_heads * head_size)
         )
     dec_att = jnp.stack(outputs).astype(jnp.bfloat16)
-    pre_rows, dec_rows = (
-        lax.all_gather(pre_att, "pool", axis=0, tiled=True),
-        lax.all_gather(dec_att, "pool", axis=1, tiled=True),
-    )
-    pre_part = jnp.dot(pre_rows, out_weight, preferred_element_type=jnp.float32)
-    dec_part = jnp.einsum("srk,kd->srd", dec_rows, out_weight, preferred_element_type=jnp.float32)
-    pre_sum, dec_sum = (
-        lax.psum_scatter(
-            pre_part.astype(jnp.bfloat16), "tensor", scatter_dimension=0, tiled=True
-        ).astype(jnp.float32),
-        lax.psum_scatter(
-            dec_part.astype(jnp.bfloat16), "tensor", scatter_dimension=1, tiled=True
-        ).astype(jnp.float32),
-    )
-    return (pre_sum.astype(jnp.bfloat16), dec_sum.astype(jnp.bfloat16), arrived)
+    dec_count = 2 * request_count
+    att = jnp.concatenate([dec_att.reshape(dec_count, -1), pre_att], axis=0)
+    half = row_count // 2
+    chunks = ((0, dec_count), (dec_count, half), (dec_count + half, half))
+    projected = project_all(att, out_weight, chunks)
+    slot_members, _, columns = projected.shape
+    pre_sum = projected[:, dec_count:].reshape(slot_members * row_count, columns)
+    dec_sum = (
+        projected[:, :dec_count]
+        .reshape(slot_members, 2, request_count, columns)
+        .transpose(1, 0, 2, 3)
+        .reshape(2, slot_members * request_count, columns)
+    )
+    return (pre_sum, dec_sum, arrived)
 
 
 def solution(mesh):

time: 226 us -> 177 us (0.78)
  Pallas kernels: 0 us -> 98.1 us
  waiting for transfers between devices: 78.6 us -> 7.7 us
  blocking collectives: 50.7 us -> 0 us
  matrix products: 46 us -> 25.8 us
    pallas_call x0 -> x1, Pallas kernels: none -> 98.1 us  [project_all(): pl.pallas_call(functools.partial(project_kernel, chunks, slot_members), o...]
    all_gather x1 -> x0, blocking collectives: 33.3 us -> none  [body(): lax.all_gather(dec_att, 'pool', axis=1, tiled=True)]
    all_gather x1 -> x0, waiting for transfers between devices: 31.3 us -> none  [body(): lax.all_gather(pre_att, 'pool', axis=0, tiled=True)]
    reduce_scatter x1 -> x0, waiting for transfers between devices: 20.2 us -> none  [body(): lax.psum_scatter(pre_part.astype(jnp.bfloat16), 'tensor', scatter_dimensi...]
    all_gather x1, waiting for transfers between devices: 27 us -> 7.68 us  [body(): key_piece = lax.all_gather(prompt_key_value, 'pool', axis=0, tiled=True)]
    dot_general x3 -> x1, matrix products: 19.6 us -> 0.29 us  [body(): jnp.einsum('pcb,pbf->pcf', select_entries, key_piece.reshape(pool_size, b...]
    all_to_all x1 -> x0, blocking collectives: 17.4 us -> none  [body(): lax.all_to_all(outgoing, 'pool', split_axis=0, concat_axis=0, tiled=True)]
    unnamed x23 -> x21, local copies, waits for them, and re-layouts: 9.77 us -> 3.84 us
  transfers between devices with their start and end apart: 4 -> 1, of which waited for: 3 -> 1; matrix products, arithmetic and copies ran while one was open for 23% -> 14% of each run, Pallas kernels for 0% -> 0%
where the time goes in v1:
time: 177 us
  Pallas kernels  98.1 us (55%)
  matrix products  25.8 us (15%)
  local copies, waits for them, and re-layouts  19.3 us (11%)
  between operations  14.3 us (8%)
  other arithmetic  11.8 us (7%)
  waiting for transfers between devices  7.7 us (4%)
    pallas_call x1, Pallas kernels, project_all(): pl.pallas_call(functools.partial(project_kernel, chunks, slot_members), o...  98.1 us
    slice x1, local copies, waits for them, and re-layouts, body(): old_keys = dec_cache[..., :head_size]  10.1 us
    reduce_sum x1, other arithmetic, body(): new_sum = jnp.sum(weights, axis=-1)  9.2 us
    dot_general x1, matrix products, body(): jnp.einsum('thgd,shd->thgs', query_matrix, key_piece[..., :head_size], pr...  8.3 us
    dot_general x1, matrix products, body(): jnp.einsum('thgs,shd->thgd', weights.astype(jnp.bfloat16), key_piece[...,...  7.73 us
    all_gather x1, waiting for transfers between devices, body(): key_piece = lax.all_gather(prompt_key_value, 'pool', axis=0, tiled=True)  7.68 us
    dot_general x2, matrix products, body(): jnp.einsum('rhgc,rchd->rhgd', old_weights.astype(jnp.bfloat16), old_value...  4.87 us
    dot_general x2, matrix products, body(): jnp.einsum('rhgd,rchd->rhgc', query_rows, old_keys, preferred_element_typ...  3.94 us
  transfers between devices with their start and end apart: 1, of which 1 were waited for; matrix products, arithmetic and copies ran while one was open for 14% of the time, Pallas kernels for 0%

profile of v1, /device:TPU:0, one launch (start us, length us, event | category | flops | bytes accessed | tf_op | source)
XLA Modules:
  0.0 177.1 jit_solution(18268936132418553022)
XLA Ops:
  7.2 1.7 copy.37
  8.9 0.7 bitcast_convert_fusion
  9.7 0.8 fusion.69
  10.5 10.1 %fusion.68 = (bf16[24,512,2,128]{3,2,1,0:T(2,128)(2,1)S(1)}, bf16[24,512,2,128]{3,2,1,0:T(2,128)(2,1)S(1)}) fusion(bf16[24,512,2,256]{3,2,1,0:T(2,128)(2,1)} %param.15), kind=kLoop, calls=%fused_computation.82 | loop fusion | bytes 25165824 | tf_op jit(solution)/shard_map/slice | solution.py:328
  20.8 0.2 fusion.57
  21.0 1.9 %select_reduce_fusion.1 = (f32[24,2,8]{2,1,0:T(2,128)S(1)}, f32[24,2,8,512]{3,2,1,0:T(8,128)S(1)}) fusion(pred[24,512]{1,0:T(8,128)(4,1)S(1)} %iota_compare_fusion.1, bf16[24,2,8,128]{3,2,1,0:T(8,128)(2,1)S(1)} %bitcast.75, bf16[24,512,2,128]{3,2,1,0:T(2,128)(2,1)S(1)} %get-tuple-element.14), kind=kOutput, calls=%fused_computation.38 | convolution fusion | flops 50921088 | bytes 7190016 | tf_op jit(solution)/shard_map/rhgd,rchd->rhgc/dot_general | solution.py:336
  22.9 0.2 fusion.70
  23.1 2.0 %fusion.39 = (f32[24,2,8]{2,1,0:T(2,128)S(1)}, f32[24,2,8]{2,1,0:T(2,128)S(1)}, f32[24,2,8,512]{3,2,1,0:T(8,128)S(1)}) fusion(f32[24,2,8,512]{3,2,1,0:T(8,128)S(1)} %get-tuple-element.27, f32[24,2,8]{2,1,0:T(2,128)S(1)} %multiply_maximum_fusion, pred[24,512]{1,0:T(8,128)(4,1)S(1)} %iota_compare_fusion.1, bf16[24,2,8,128]{3,2,1,0:T(8,128)(2,1)S(1)} %bitcast.78, ...), kind=kOutput, calls=%fused_computation.39 | convolution fusion | flops 51510528 | bytes 7979520 | tf_op jit(solution)/shard_map/rhgd,rchd->rhgc/dot_general | solution.py:336
  25.2 0.3 fusion.41
  25.5 1.0 fusion.8
  26.6 0.1 fusion.51
  26.7 0.3 fusion.29
  27.1 0.2 copy.58
  27.4 3.8 %fusion.33 = bf16[24,2,8,128]{3,2,1,0:T(8,128)(2,1)S(1)} fusion(bf16[24,512,2,128]{3,2,1,0:T(2,128)(2,1)} %copy-done, f32[24,2,8,512]{3,2,1,0:T(8,128)S(1)} %get-tuple-element.27, f32[24,2,8]{2,1,0:T(2,128)S(1)} %multiply_maximum_fusion, pred[24,512]{1,0:T(8,128)(4,1)S(1)} %iota_compare_fusion.1, f32[24,2,8]{2,1,0:T(2,128)S(1)} %get-tuple-element.19, ...), kind=kOutput, calls=%fused_computation.29 | convolution fusion | flops 51118080 | bytes 7217664 | tf_op jit(solution)/shard_map/rhgc,rchd->rhgd/dot_general | solution.py:355
  31.2 0.5 broadcast.69
  31.8 0.7 reduce.3
  32.4 0.1 broadcast_in_dim_reshape_squeeze.2
  32.6 0.2 select_reduce_fusion.2
  32.9 0.3 fusion.38
  33.1 7.7 %all-gather.2.cloned.1.call-done = bf16[1024,2,256]{2,0,1:T(8,128)(2,1)} async-done(((bf16[256,2,256]{2,0,1:T(8,128)(2,1)}), bf16[1024,2,256]{2,0,1:T(8,128)(2,1)}) %all-gather.2.cloned.1.call-update) | async-done | bytes 1048592 | tf_op jit(solution)/shard_map/all_gather | solution.py:279
  40.8 8.3 %fusion = (f32[256,2,8]{0,2,1:T(8,128)S(1)}, f32[2,1024,256,8]{2,1,3,0:T(8,128)}) fusion(pred[256,1024]{0,1:T(8,128)(4,1)S(1)} %fusion.38, bf16[256,2,8,128]{3,2,1,0:T(8,128)(2,1)S(1)} %bitcast.69, bf16[1024,2,256]{2,0,1:T(8,128)(2,1)} %all-gather.2.cloned.1.call-done), kind=kOutput, calls=%fused_computation.2 | convolution fusion | flops 1086320640 | bytes 18628608 | tf_op jit(solution)/shard_map/thgd,shd->thgs/dot_general | solution.py:283
  49.1 9.2 %fusion.3 = f32[256,2,8]{0,2,1:T(8,128)S(1)} fusion(f32[2,1024,256,8]{2,1,3,0:T(8,128)} %get-tuple-element.25, f32[256,2,8]{0,2,1:T(8,128)S(1)} %broadcast_maximum_fusion, pred[256,1024]{0,1:T(8,128)(4,1)S(1)} %fusion.38), kind=kLoop, calls=%fused_computation.5 | loop fusion | flops 16773120 | bytes 17072128 | tf_op jit(solution)/shard_map/reduce_sum | solution.py:299
  58.3 7.7 %fusion.16 = bf16[256,2,8,128]{0,3,2,1:T(8,128)(2,1)S(1)} fusion(f32[2,1024,256,8]{2,1,3,0:T(8,128)} %get-tuple-element.25, f32[256,2,8]{0,2,1:T(8,128)S(1)} %broadcast_maximum_fusion, pred[256,1024]{0,1:T(8,128)(4,1)S(1)} %fusion.38, f32[256,2,8]{0,2,1:T(8,128)S(1)} %fusion.3, bf16[1024,2,256]{2,0,1:T(8,128)(2,1)S(1)} %copy-done.1), kind=kOutput, calls=%fused_computation.19 | convolution fusion | flops 1091567616 | bytes 18644992 | tf_op jit(solution)/shard_map/thgs,shd->thgd/dot_general | solution.py:300
  66.1 0.6 copy.51
  66.7 0.1 pad_maximum_fusion.att_ref
  66.8 98.1 %shard_map.112 = bf16[1,304,2048]{2,1,0:T(8,128)(2,1)S(1)} custom-call(bf16[304,2048]{1,0:T(8,128)(2,1)S(1)} %pad_maximum_fusion.att_ref, bf16[2048,2048]{1,0:T(8,128)(2,1)} %weight_ref.1), custom_call_target="tpu_custom_call" | custom-call | flops 10200547328 | bytes 10878976 | tf_op jit(solution)/shard_map/pallas_call | solution.py:210
  164.9 1.1 slice_bitcast_fusion
  166.0 0.7 slice.47
  166.7 1.1 copy.42
  167.8 0.8 reshape.153
  168.6 0.3 convolution_convert_fusion
  168.9 1.3 copy.43
  (32 shorter events, 0.5 us)
Async XLA Ops:
  7.2 33.6 %all-gather.2.cloned.1.call-start = ((), (), s32[]{:S(2)}) async-start(), calls=%async_computation | async-start | bytes 1310720 | tf_op jit(solution)/shard_map/all_gather | solution.py:279
  10.5 10.1 %copy-start.5 = (s32[24]{0:T(128)S(1)}, s32[24]{0:T(128)}, u32[]{:S(2)}) copy-start(s32[24]{0:T(128)} %param.16) | copy-start | bytes 292
  10.5 10.2 %copy-start.3 = (bf16[2,24,2048]{2,1,0:T(8,128)(2,1)S(1)}, bf16[2,24,2048]{2,1,0:T(8,128)(2,1)}, u32[]{:S(2)}) copy-start(bf16[2,24,2048]{2,1,0:T(8,128)(2,1)} %param.13) | copy-start | bytes 589828
  20.6 4.9 %copy-start = (bf16[24,512,2,128]{3,2,1,0:T(2,128)(2,1)}, bf16[24,512,2,128]{3,2,1,0:T(2,128)(2,1)S(1)}, u32[]{:S(2)}) copy-start(bf16[24,512,2,128]{3,2,1,0:T(2,128)(2,1)S(1)} %get-tuple-element.15) | copy-start | bytes 18874372
  25.2 1.9 %copy-start.2 = (bf16[256,2048]{1,0:T(8,128)(2,1)S(1)}, bf16[256,2048]{1,0:T(8,128)(2,1)}, u32[]{:S(2)}) copy-start(bf16[256,2048]{1,0:T(8,128)(2,1)} %param.9) | copy-start | bytes 3145732
  26.7 5.1 %copy-start.6 = (s32[64,1]{0,1:T(1,128)S(1)}, s32[64,1]{0,1:T(1,128)}, u32[]{:S(2)}) copy-start(s32[64,1]{0,1:T(1,128)} %param.12) | copy-start | bytes 772
  26.7 5.8 %copy-start.4 = (s32[1024]{0:T(1024)S(1)}, s32[1024]{0:T(1024)}, u32[]{:S(2)}) copy-start(s32[1024]{0:T(1024)} %param.11) | copy-start | bytes 12292
  49.1 9.2 %copy-start.1 = (bf16[1024,2,256]{2,0,1:T(8,128)(2,1)S(1)}, bf16[1024,2,256]{2,0,1:T(8,128)(2,1)}, u32[]{:S(2)}) copy-start(bf16[1024,2,256]{2,0,1:T(8,128)(2,1)} %all-gather.2.cloned.1.call-done) | copy-start | bytes 3145732
Sparse Core Ops, SparseCore 0:
  10.1 30.6 all-gather.1

commit v2 on v1

v2 whole, which is shorter than its diff:
```python
import functools
import math

import jax
import jax.numpy as jnp
from jax import lax
from jax.experimental import pallas as pl
from jax.experimental.pallas import tpu as pltpu
from jax.sharding import PartitionSpec as P

BLOCK_TOKENS = 16
MESH = pl.DeviceIdType.MESH
COLUMN_TILE = 512


def inner(rows, keys):
    return lax.dot_general(
        rows, keys, (((1,), (1,)), ((), ())), preferred_element_type=jnp.float32
    )


def layer_kernel(
    chunks,
    slot_members,
    scale,
    query_ref,
    kv_ref,
    bias_ref,
    dec_query_ref,
    dec_new_ref,
    ctx_ref,
    pick_ref,
    cache_ref,
    weight_ref,
    pre_ref,
    dec_ref,
    arrived_ref,
    gathered,
    weight,
    outgoing,
    landed,
    total,
    cache,
    held,
    query,
    dec_rows,
    load_sem,
    cache_sem,
    kv_send,
    kv_recv,
    ring_send,
    ring_recv,
    part_send,
    part_recv,
):
    pool = lax.axis_size("pool")
    tensor = lax.axis_size("tensor")
    group = lax.axis_index("groups")
    me = lax.axis_index("pool")
    lane = lax.axis_index("tensor")
    columns = weight_ref.shape[1]
    tile = min(COLUMN_TILE, columns)
    has_left = me > 0
    has_right = me < pool - 1

    requests = cache_ref.shape[0]
    kv_heads = kv_ref.shape[0]
    head_size = kv_ref.shape[-1] // 2
    group_size = query_ref.shape[1] // (kv_heads * head_size)
    back = held.shape[0] - pool
    dec_count = chunks[0][1]

    load_kv = pltpu.make_async_copy(kv_ref, held.at[back + me], load_sem.at[0])
    load_kv.start()

    @pl.loop(0, requests)
    def _(request):
        pltpu.make_async_copy(
            cache_ref.at[request], cache.at[request], cache_sem.at[request]
        ).start()

    load_query = pltpu.make_async_copy(query_ref, query, load_sem.at[1])
    load_query.start()
    load_weight = pltpu.make_async_copy(weight_ref, weight, load_sem.at[2])
    load_weight.start()
    for place in range(back):
        held[place] = jnp.zeros(held.shape[1:], held.dtype)

    barrier = pltpu.get_barrier_semaphore()

    @pl.when(has_left)
    def _():
        pl.semaphore_signal(barrier, inc=1, device_id=(group, me - 1, lane), device_id_type=MESH)

    @pl.when(has_right)
    def _():
        pl.semaphore_signal(barrier, inc=1, device_id=(group, me + 1, lane), device_id_type=MESH)

    for step in range(1, tensor):
        peer = lax.rem(lane + step, tensor)
        pl.semaphore_signal(barrier, inc=1, device_id=(group, me, peer), device_id_type=MESH)

    pl.semaphore_wait(
        barrier, has_left.astype(jnp.int32) + has_right.astype(jnp.int32) + tensor - 1
    )

    def ring_copy(member, chunk, way):
        start, size = chunks[chunk]
        block = gathered.at[member, pl.ds(start, size)]
        return pltpu.make_async_remote_copy(
            src_ref=block,
            dst_ref=block,
            send_sem=ring_send.at[way, member, chunk],
            recv_sem=ring_recv.at[member, chunk],
            device_id=(group, me - 1 if way == 0 else me + 1, lane),
            device_id_type=MESH,
        )

    def part_copy(member, chunk):
        start, size = chunks[chunk]
        target = member // slot_members
        return pltpu.make_async_remote_copy(
            src_ref=outgoing.at[member, pl.ds(start, size)],
            dst_ref=landed.at[lane, member % slot_members, pl.ds(start, size)],
            send_sem=part_send.at[member, chunk],
            recv_sem=part_recv.at[lane, member % slot_members, chunk],
            device_id=(group, me, target),
            device_id_type=MESH,
        )

    def arrived_copy(source, place, chunk):
        start, size = chunks[chunk]
        return pltpu.make_async_remote_copy(
            src_ref=outgoing.at[0, pl.ds(start, size)],
            dst_ref=landed.at[source, place, pl.ds(start, size)],
            send_sem=part_send.at[0, chunk],
            recv_sem=part_recv.at[source, place, chunk],
            device_id=(group, me, source),
            device_id_type=MESH,
        )

    def project(member, chunk):
        start, size = chunks[chunk]
        mine = member // slot_members == lane

        @pl.loop(0, columns // tile)
        def _(index):
            place = pl.ds(pl.multiple_of(index * tile, tile), tile)
            part = jnp.dot(
                gathered[member, pl.ds(start, size), :],
                weight[:, place],
                preferred_element_type=jnp.float32,
            )

            @pl.when(mine)
            def _():
                total[member % slot_members, pl.ds(start, size), place] = part

            @pl.when(jnp.logical_not(mine))
            def _():
                outgoing[member, pl.ds(start, size), place] = part.astype(jnp.bfloat16)

        @pl.when(jnp.logical_not(mine))
        def _():
            part_copy(member, chunk).start()

    def kv_copy(member, way):
        block = held.at[back + member]
        return pltpu.make_async_remote_copy(
            src_ref=block,
            dst_ref=block,
            send_sem=kv_send.at[way, member],
            recv_sem=kv_recv.at[member],
            device_id=(group, me - 1 if way == 0 else me + 1, lane),
            device_id_type=MESH,
        )

    def pass_kv(distance):
        @pl.when(me - distance >= 0)
        def _():
            kv_copy(me - distance, 1).wait_recv()

            @pl.when(has_right)
            def _():
                kv_copy(me - distance, 1).start()

        @pl.when(me + distance < pool)
        def _():
            kv_copy(me + distance, 0).wait_recv()

            @pl.when(has_left)
            def _():
                kv_copy(me + distance, 0).start()

    def send_own(chunk):
        @pl.when(has_left)
        def _():
            ring_copy(me, chunk, 0).start()

        @pl.when(has_right)
        def _():
            ring_copy(me, chunk, 1).start()

    load_kv.wait()

    @pl.when(has_right)
    def _():
        kv_copy(me, 1).start()

    @pl.when(has_left)
    def _():
        kv_copy(me, 0).start()

    @pl.loop(0, requests)
    def _(request):
        for distance in range(1, back + 1):
            @pl.when(request == requests * distance // (back + 1))
            def _():
                pass_kv(distance)

        pltpu.make_async_copy(
            cache_ref.at[request], cache.at[request], cache_sem.at[request]
        ).wait()
        if len(cache.shape) == 4:
            slots = cache.shape[1] * cache.shape[2]
            keys = cache[request, :, :, 0:head_size].reshape(slots, head_size)
            values = cache[request, :, :, head_size:].reshape(slots, head_size)
        else:
            slots = cache.shape[1]
            keys = cache[request, :, 0:head_size]
            values = cache[request, :, head_size:]
        rows = dec_query_ref[request]
        new_keys = dec_new_ref[request, :, 0:head_size]
        new_values = dec_new_ref[request, :, head_size:]
        row = lax.broadcasted_iota(jnp.int32, (rows.shape[0], 1), 0)
        row_head = (row // group_size) % kv_heads
        row_step = row // (group_size * kv_heads)
        slot = lax.broadcasted_iota(jnp.int32, (1, slots), 1)
        new_slot = lax.broadcasted_iota(jnp.int32, (1, new_keys.shape[0]), 1)
        live = (slot % kv_heads == row_head) & (slot < ctx_ref[request] * kv_heads)
        new_live = (new_slot % kv_heads == row_head) & (new_slot // kv_heads <= row_step)
        scores = jnp.where(live, inner(rows, keys) * scale, -1e30)
        new_scores = jnp.where(new_live, inner(rows, new_keys) * scale, -1e30)
        most = jnp.maximum(
            jnp.max(scores, axis=-1, keepdims=True), jnp.max(new_scores, axis=-1, keepdims=True)
        )
        weights = jnp.exp(scores - most)
        new_weights = jnp.exp(new_scores - most)
        amount = jnp.sum(weights, axis=-1, keepdims=True) + jnp.sum(
            new_weights, axis=-1, keepdims=True
        )
        mixed = jnp.dot(
            weights.astype(jnp.bfloat16), values, preferred_element_type=jnp.float32
        ) + jnp.dot(
            new_weights.astype(jnp.bfloat16), new_values, preferred_element_type=jnp.float32
        )
        dec_rows[request] = mixed / amount

    heads = kv_heads * group_size
    for head in range(heads):
        both = jnp.concatenate([dec_rows[:, head, :], dec_rows[:, heads + head, :]], axis=0)
        gathered[me, 0:dec_count, head * head_size : (head + 1) * head_size] = both.astype(
            jnp.bfloat16
        )
    send_own(0)

    load_query.wait()
    for chunk in range(1, len(chunks)):
        start, size = chunks[chunk]
        first = start - dec_count
        for kv_head in range(kv_heads):
            @pl.loop(0, group_size // 2)
            def _(pair):
                column = pl.multiple_of(
                    (kv_head * group_size + 2 * pair) * head_size, 2 * head_size
                )
                wide = query[pl.ds(first, size), pl.ds(column, 2 * head_size)]
                rows = jnp.concatenate([wide[:, :head_size], wide[:, head_size:]], axis=0)
                bias = bias_ref[pl.ds(first, size), :]
                scores = jnp.concatenate(
                    [
                        inner(rows, held[me + place, kv_head, :, :, 0:head_size].reshape(-1, head_size))
                        for place in range(back + 1)
                    ],
                    axis=1,
                ) * scale + jnp.concatenate([bias, bias], axis=0)
                weights = jnp.exp(scores - jnp.max(scores, axis=-1, keepdims=True))
                amount = jnp.sum(weights, axis=-1, keepdims=True)
                weights = weights.astype(jnp.bfloat16)
                width = bias.shape[1] // (back + 1)
                mixed = jnp.zeros(rows.shape, jnp.float32)
                for place in range(back + 1):
                    mixed = mixed + jnp.dot(
                        weights[:, place * width : (place + 1) * width],
                        held[me + place, kv_head, :, :, head_size:].reshape(-1, head_size),
                        preferred_element_type=jnp.float32,
                    )
                mixed = (mixed / amount).astype(jnp.bfloat16)
                gathered[me, pl.ds(start, size), pl.ds(column, 2 * head_size)] = jnp.concatenate(
                    [mixed[:size], mixed[size:]], axis=1
                )
        send_own(chunk)

    load_weight.wait()

    @pl.loop(0, pool)
    def _(distance):
        left = me - distance
        right = me + distance
        use_left = left >= 0
        use_right = jnp.logical_and(right < pool, distance > 0)

        @pl.when(distance > back)
        def _():
            pass_kv(distance)

        for chunk in range(len(chunks)):
            @pl.when(jnp.logical_and(use_left, distance > 0))
            def _():
                ring_copy(left, chunk, 1).wait_recv()

                @pl.when(has_right)
                def _():
                    ring_copy(left, chunk, 1).start()

            @pl.when(use_right)
            def _():
                ring_copy(right, chunk, 0).wait_recv()

                @pl.when(has_left)
                def _():
                    ring_copy(right, chunk, 0).start()

            @pl.when(use_left)
            def _():
                project(left, chunk)

            @pl.when(use_right)
            def _():
                project(right, chunk)

    capacity = arrived_ref.shape[1]

    @pl.loop(0, pool)
    def _(source):
        for slot in range(capacity):
            choice = pick_ref[source * capacity + slot]
            for kv_head in range(kv_heads):
                block = held[back + source, kv_head, jnp.maximum(choice, 0)]
                arrived_ref[source, slot, kv_head] = jnp.where(
                    choice >= 0, block, jnp.zeros_like(block)
                )

    for place in range(slot_members):
        for chunk in range(len(chunks)):
            start, size = chunks[chunk]
            for step in range(1, tensor):
                arrived_copy(lax.rem(lane + step, tensor), place, chunk).wait_recv()

            @pl.loop(0, columns // tile)
            def _(index):
                span = pl.ds(pl.multiple_of(index * tile, tile), tile)
                value = total[place, pl.ds(start, size), span]
                for step in range(1, tensor):
                    source = lax.rem(lane + step, tensor)
                    value = value + landed[source, place, pl.ds(start, size), span].astype(
                        jnp.float32
                    )
                if chunk == 0:
                    dec_ref[place, :, span] = value.astype(jnp.bfloat16)
                else:
                    pre_ref[place, pl.ds(start - dec_count, size), span] = value.astype(
                        jnp.bfloat16
                    )

    @pl.loop(0, pool)
    def _(member):
        for chunk in range(len(chunks)):
            @pl.when(jnp.logical_and(has_left, member >= me))
            def _():
                if chunk == 0:
                    kv_copy(member, 0).wait_send()
                ring_copy(member, chunk, 0).wait_send()

            @pl.when(jnp.logical_and(has_right, member <= me))
            def _():
                if chunk == 0:
                    kv_copy(member, 1).wait_send()
                ring_copy(member, chunk, 1).wait_send()

            @pl.when(member // slot_members != lane)
            def _():
                part_copy(member, chunk).wait_send()


def attend_and_project(
    prompt_query, kv_blocks, bias, dec_query, dec_new, ctx_len, picks, dec_cache, out_weight,
    chunks, scale
):
    pool = lax.axis_size("pool")
    tensor = lax.axis_size("tensor")
    row_count, depth = prompt_query.shape
    rows = sum(size for _, size in chunks)
    columns = out_weight.shape[1]
    slot_members = pool // tensor
    count = len(chunks)
    back = bias.shape[1] // row_count - 1
    kv_heads, _, block_size, width = kv_blocks.shape
    requests = dec_cache.shape[0]
    capacity = picks.shape[0] // pool
    vmem = pl.BlockSpec(memory_space=pltpu.VMEM)
    smem = pl.BlockSpec(memory_space=pltpu.SMEM)
    hbm = pl.BlockSpec(memory_space=pl.ANY)
    return pl.pallas_call(
        functools.partial(layer_kernel, chunks, slot_members, scale),
        out_shape=(
            jax.ShapeDtypeStruct((slot_members, row_count, columns), jnp.bfloat16),
            jax.ShapeDtypeStruct((slot_members, chunks[0][1], columns), jnp.bfloat16),
            jax.ShapeDtypeStruct((pool, capacity, kv_heads, block_size, width), jnp.bfloat16),
        ),
        in_specs=[hbm, hbm, vmem, vmem, vmem, smem, smem, hbm, hbm],
        out_specs=(vmem, vmem, vmem),
        scratch_shapes=[
            pltpu.VMEM((pool, rows, depth), jnp.bfloat16),
            pltpu.VMEM((depth, columns), jnp.bfloat16),
            pltpu.VMEM((pool, rows, columns), jnp.bfloat16),
            pltpu.VMEM((tensor, slot_members, rows, columns), jnp.bfloat16),
            pltpu.VMEM((slot_members, rows, columns), jnp.float32),
            pltpu.VMEM(dec_cache.shape, jnp.bfloat16),
            pltpu.VMEM((back + pool,) + kv_blocks.shape, jnp.bfloat16),
            pltpu.VMEM(prompt_query.shape, jnp.bfloat16),
            pltpu.VMEM(dec_query.shape, jnp.float32),
            pltpu.SemaphoreType.DMA((3,)),
            pltpu.SemaphoreType.DMA((requests,)),
            pltpu.SemaphoreType.DMA((2, pool)),
            pltpu.SemaphoreType.DMA((pool,)),
            pltpu.SemaphoreType.DMA((2, pool, count)),
            pltpu.SemaphoreType.DMA((pool, count)),
            pltpu.SemaphoreType.DMA((pool, count)),
            pltpu.SemaphoreType.DMA((tensor, slot_members, count)),
        ],
        compiler_params=pltpu.CompilerParams(
            collective_id=0, has_side_effects=True, vmem_limit_bytes=58 * 1024 * 1024
        ),
    )(prompt_query, kv_blocks, bias, dec_query, dec_new, ctx_len, picks, dec_cache, out_weight)


def block_ranks(destinations):
    item_count = destinations.shape[-1]
    same_dest = destinations[..., :, None] == destinations[..., None, :]
    earlier = (
        jnp.arange(item_count, dtype=jnp.int32)[None, :]
        < jnp.arange(item_count, dtype=jnp.int32)[:, None]
    )
    return jnp.sum(jnp.where(same_dest & earlier, 1, 0), axis=-1).astype(jnp.int32)


def body(
    prompt_query,
    prompt_key_value,
    segment_ids,
    block_dest,
    decode_query,
    dec_kv,
    dec_cache,
    ctx_len,
    out_weight,
):
    row_count = prompt_query.shape[0]
    kv_heads = prompt_key_value.shape[1]
    head_size = prompt_key_value.shape[2] // 2
    query_heads = prompt_query.shape[1] // head_size
    group_size = query_heads // kv_heads
    scale = 1.0 / math.sqrt(head_size)
    pool_size = lax.axis_size("pool")
    my_index = lax.axis_index("pool")
    block_count = row_count // BLOCK_TOKENS
    capacity = max(2, 2 * block_count // pool_size)
    request_count = decode_query.shape[1]
    cache_length = dec_cache.shape[1]
    kv_blocks = prompt_key_value.transpose(1, 0, 2).reshape(
        kv_heads, block_count, BLOCK_TOKENS, 2 * head_size
    )

    most = pool_size * row_count // 2
    back = -(-(most - 1) // row_count)
    own_start = my_index * row_count
    own_positions = own_start + jnp.arange(row_count, dtype=jnp.int32)
    own_segments = lax.dynamic_slice_in_dim(segment_ids, own_start, row_count, 0)
    window = (back + 1) * row_count
    key_positions = own_start - back * row_count + jnp.arange(window, dtype=jnp.int32)
    padded = jnp.concatenate([jnp.full((back * row_count,), -1, jnp.int32), segment_ids])
    key_segments = lax.dynamic_slice_in_dim(padded, own_start, window, 0)
    allowed = (own_segments[:, None] == key_segments[None, :]) & (
        key_positions[None, :] <= own_positions[:, None]
    )
    bias = jnp.where(allowed, 0.0, -1e30).astype(jnp.float32)

    destinations = block_dest[:, 0].reshape(pool_size, block_count)
    slot_ranks = block_ranks(destinations)
    slot_ids = jnp.arange(capacity, dtype=jnp.int32)
    chosen = (destinations[:, None, :] == my_index) & (
        slot_ranks[:, None, :] == slot_ids[None, :, None]
    )
    picks = jnp.max(
        jnp.where(chosen, jnp.arange(block_count, dtype=jnp.int32)[None, None, :], -1), axis=-1
    ).reshape(-1)

    dec_query = (
        decode_query.reshape(2, request_count, query_heads, head_size)
        .transpose(1, 0, 2, 3)
        .reshape(request_count, 2 * query_heads, head_size)
    )
    dec_new = dec_kv.transpose(1, 0, 2, 3).reshape(request_count, 2 * kv_heads, 2 * head_size)
    dec_new = jnp.pad(dec_new, ((0, 0), (0, 16 - 2 * kv_heads), (0, 0)))
    if kv_heads == 1:
        dec_cache = dec_cache.reshape(request_count, cache_length, 2 * head_size)
    dec_count = 2 * request_count
    half = row_count // 2
    chunks = ((0, dec_count), (dec_count, half), (dec_count + half, half))
    pre, dec, arrived = attend_and_project(
        prompt_query, kv_blocks, bias, dec_query, dec_new, ctx_len, picks, dec_cache, out_weight,
        chunks, scale
    )
    slot_members, _, columns = pre.shape
    return (
        pre.reshape(slot_members * row_count, columns),
        dec.reshape(slot_members, 2, request_count, columns)
        .transpose(1, 0, 2, 3)
        .reshape(2, slot_members * request_count, columns),
        arrived.transpose(0, 1, 3, 2, 4)[None],
    )


def solution(mesh):
    return jax.shard_map(
        body,
        mesh=mesh,
        in_specs=(
            P(("groups", "pool"), "tensor"),
            P(("groups", "pool"), "tensor", None),
            P("groups"),
            P("groups", None),
            P(None, ("groups", "pool"), "tensor"),
            P(None, ("groups", "pool"), "tensor", None),
            P(("groups", "pool"), None, "tensor", None),
            P(("groups", "pool")),
            P("tensor", "pool"),
        ),
        out_specs=(
            P(("groups", "tensor"), "pool"),
            P(None, ("groups", "tensor"), "pool"),
            P(("groups", "pool"), None, None, None, "tensor", None),
        ),
        check_vma=False,
    )
```

time: 177 us -> 140 us (0.79)
  matrix products: 25.8 us -> 0 us
  Pallas kernels: 98.1 us -> 122 us
  between operations: 14.3 us -> 0.66 us
  other arithmetic: 11.8 us -> 3.53 us
  waiting for transfers between devices: 7.7 us -> 0 us
  local copies, waits for them, and re-layouts: 19.3 us -> 13.1 us
    dot_general x10 -> x0, matrix products: 25.8 us -> none  [the longest x1 8.3 us: body(): jnp.einsum('thgd,shd->thgs', query_matrix, key_piece[..., :head_size], pr...]
    pallas_call x1, Pallas kernels: 98.1 us -> 122 us  [attend_and_project(): pl.pallas_call(functools.partial(layer_kernel, chunks, slot_members, scal...]
    slice x3 -> x0, local copies, waits for them, and re-layouts: 11.6 us -> none  [the longest x1 10.1 us: body(): old_keys = dec_cache[..., :head_size]]
    reduce_sum x3 -> x0, other arithmetic: 9.64 us -> none  [the longest x1 9.2 us: body(): new_sum = jnp.sum(weights, axis=-1)]
    all_gather x1 -> x0, waiting for transfers between devices: 7.68 us -> none  [body(): key_piece = lax.all_gather(prompt_key_value, 'pool', axis=0, tiled=True)]
    unnamed x21 -> x5, local copies, waits for them, and re-layouts: 3.84 us -> 7.74 us
    transpose x0 -> x2, local copies, waits for them, and re-layouts: none -> 2.51 us  [the longest x1 1.68 us: body(): prompt_key_value.transpose(1, 0, 2)]
  transfers between devices with their start and end apart: 1 -> 0, of which waited for: 1 -> 0; matrix products, arithmetic and copies ran while one was open for 14% -> 0% of each run, Pallas kernels for 0% -> 0%
where the time goes in v2:
time: 140 us; the launch traced here: 139 us
  Pallas kernels  122 us (87%)
  local copies, waits for them, and re-layouts  13.1 us (9%)
  other arithmetic  3.53 us (3%)
    pallas_call x1, Pallas kernels, attend_and_project(): pl.pallas_call(functools.partial(layer_kernel, chunks, slot_members, scal...  122 us
    unnamed x5, local copies, waits for them, and re-layouts  7.74 us

profile of v2, /device:TPU:0, one launch (start us, length us, event | category | flops | bytes accessed | tf_op | source)
XLA Modules:
  0.0 139.3 jit_solution(2710185712309989968)
XLA Ops:
  0.6 0.5 broadcast.28
  1.1 1.3 reduce.3
  2.5 0.8 dynamic_slice.6
  3.2 0.1 broadcast_in_dim_reshape_squeeze.2
  3.3 0.2 select_reduce_fusion
  3.5 0.2 select_reduce_fusion.1
  3.7 0.6 reshape.60.pick_ref
  4.3 0.8 pad_dynamic-slice_fusion
  5.1 0.8 copy.18
  6.0 0.7 pad.5.dec_new_ref
  6.7 1.0 copy.20
  7.6 0.7 copy.17
  8.3 1.7 %copy.16 = bf16[2,256,256]{2,1,0:T(8,128)(2,1)} copy(bf16[2,256,256]{2,0,1:T(2,128)(2,1)} %bitcast.21) | data formatting | bytes 524288 | tf_op jit(solution)/shard_map/transpose | solution.py:481
  10.0 1.1 and_select_fusion.bias_ref
  11.0 121.9 %shard_map.112 = (bf16[1,256,2048]{2,1,0:T(8,128)(2,1)}, bf16[1,48,2048]{2,1,0:T(8,128)(2,1)}, bf16[4,8,2,16,256]{4,3,2,1,0:T(8,128)(2,1)}) custom-call(bf16[256,2048]{1,0:T(8,128)(2,1)} %query_ref.1, bf16[2,16,16,256]{3,2,1,0:T(8,128)(2,1)} %bitcast.16, f32[256,768]{1,0:T(8,128)} %and_select_fusion.bias_ref, bf16[24,32,128]{2,1,0:T(8,128)(2,1)} %bitcast.18, ...), custom_call_target="tpu_custom_call" | custom-call | tf_op jit(solution)/shard_map/pallas_call | solution.py:414
  133.0 2.4 %copy.19 = bf16[1,4,8,16,2,256]{5,4,3,2,1,0:T(2,128)(2,1)} copy(bf16[1,4,8,16,2,256]{5,3,4,2,1,0:T(8,128)(2,1)} %bitcast.20) | data formatting | bytes 1048576
  135.3 2.3 %copy.23 = bf16[256,2048]{1,0:T(8,128)(2,1)} copy(bf16[256,2048]{1,0:T(8,128)(2,1)} %bitcast.17) | data formatting | bytes 2097152
  137.7 1.6 %copy.24 = bf16[2,24,2048]{2,1,0:T(8,128)(2,1)} copy(bf16[2,24,2048]{2,1,0:T(8,128)(2,1)} %bitcast.23) | data formatting | bytes 393216
  (4 shorter events, 0.1 us)

commit v3 on v2

--- a/solution.py
+++ b/solution.py
@@ -68,7 +68,8 @@
     head_size = kv_ref.shape[-1] // 2
     group_size = query_ref.shape[1] // (kv_heads * head_size)
     back = held.shape[0] - pool
-    dec_count = chunks[0][1]
+    dec_chunk = len(chunks) - 1
+    dec_start, dec_count = chunks[dec_chunk]
 
     load_kv = pltpu.make_async_copy(kv_ref, held.at[back + me], load_sem.at[0])
     load_kv.start()
@@ -211,13 +212,7 @@
     def _():
         kv_copy(me, 0).start()
 
-    @pl.loop(0, requests)
-    def _(request):
-        for distance in range(1, back + 1):
-            @pl.when(request == requests * distance // (back + 1))
-            def _():
-                pass_kv(distance)
-
+    def attend_request(request):
         pltpu.make_async_copy(
             cache_ref.at[request], cache.at[request], cache_sem.at[request]
         ).wait()
@@ -256,27 +251,29 @@
         )
         dec_rows[request] = mixed / amount
 
-    heads = kv_heads * group_size
-    for head in range(heads):
-        both = jnp.concatenate([dec_rows[:, head, :], dec_rows[:, heads + head, :]], axis=0)
-        gathered[me, 0:dec_count, head * head_size : (head + 1) * head_size] = both.astype(
-            jnp.bfloat16
-        )
-    send_own(0)
+    early = requests * 2 // 3
+
+    @pl.loop(0, early)
+    def _(request):
+        for distance in range(1, back + 1):
+            @pl.when(request == early * distance // back - 1)
+            def _():
+                pass_kv(distance)
+
+        attend_request(request)
 
     load_query.wait()
-    for chunk in range(1, len(chunks)):
+    for chunk in range(dec_chunk):
         start, size = chunks[chunk]
-        first = start - dec_count
         for kv_head in range(kv_heads):
             @pl.loop(0, group_size // 2)
             def _(pair):
                 column = pl.multiple_of(
                     (kv_head * group_size + 2 * pair) * head_size, 2 * head_size
                 )
-                wide = query[pl.ds(first, size), pl.ds(column, 2 * head_size)]
+                wide = query[pl.ds(start, size), pl.ds(column, 2 * head_size)]
                 rows = jnp.concatenate([wide[:, :head_size], wide[:, head_size:]], axis=0)
-                bias = bias_ref[pl.ds(first, size), :]
+                bias = bias_ref[pl.ds(start, size), :]
                 scores = jnp.concatenate(
                     [
                         inner(rows, held[me + place, kv_head, :, :, 0:head_size].reshape(-1, head_size))
@@ -301,6 +298,18 @@
                 )
         send_own(chunk)
 
+    @pl.loop(early, requests)
+    def _(request):
+        attend_request(request)
+
+    heads = kv_heads * group_size
+    for head in range(heads):
+        both = jnp.concatenate([dec_rows[:, head, :], dec_rows[:, heads + head, :]], axis=0)
+        gathered[me, dec_start : dec_start + dec_count, head * head_size : (head + 1) * head_size] = both.astype(
+            jnp.bfloat16
+        )
+    send_own(dec_chunk)
+
     load_weight.wait()
 
     @pl.loop(0, pool)
@@ -366,10 +375,10 @@
                     value = value + landed[source, place, pl.ds(start, size), span].astype(
                         jnp.float32
                     )
-                if chunk == 0:
+                if chunk == dec_chunk:
                     dec_ref[place, :, span] = value.astype(jnp.bfloat16)
                 else:
-                    pre_ref[place, pl.ds(start - dec_count, size), span] = value.astype(
+                    pre_ref[place, pl.ds(start, size), span] = value.astype(
                         jnp.bfloat16
                     )
 
@@ -415,7 +424,7 @@
         functools.partial(layer_kernel, chunks, slot_members, scale),
         out_shape=(
             jax.ShapeDtypeStruct((slot_members, row_count, columns), jnp.bfloat16),
-            jax.ShapeDtypeStruct((slot_members, chunks[0][1], columns), jnp.bfloat16),
+            jax.ShapeDtypeStruct((slot_members, chunks[-1][1], columns), jnp.bfloat16),
             jax.ShapeDtypeStruct((pool, capacity, kv_heads, block_size, width), jnp.bfloat16),
         ),
         in_specs=[hbm, hbm, vmem, vmem, vmem, smem, smem, hbm, hbm],
@@ -517,7 +526,7 @@
         dec_cache = dec_cache.reshape(request_count, cache_length, 2 * head_size)
     dec_count = 2 * request_count
     half = row_count // 2
-    chunks = ((0, dec_count), (dec_count, half), (dec_count + half, half))
+    chunks = ((0, half), (half, half), (row_count, dec_count))
     pre, dec, arrived = attend_and_project(
         prompt_query, kv_blocks, bias, dec_query, dec_new, ctx_len, picks, dec_cache, out_weight,
         chunks, scale

time: 140 us -> 139 us (level)
  no operation moved by 1% of the time
where the time goes in v3:
time: 139 us
  Pallas kernels  122 us (88%)
  local copies, waits for them, and re-layouts  13.1 us (9%)
  other arithmetic  3.53 us (3%)
    pallas_call x1, Pallas kernels, attend_and_project(): pl.pallas_call(functools.partial(layer_kernel, chunks, slot_members, scal...  122 us
    unnamed x5, local copies, waits for them, and re-layouts  7.74 us

profile of v3, /device:TPU:0, one launch (start us, length us, event | category | flops | bytes accessed | tf_op | source)
XLA Modules:
  0.0 138.9 jit_solution(17357999447033945028)
XLA Ops:
  0.6 0.5 broadcast.28
  1.1 1.3 reduce.3
  2.5 0.8 dynamic_slice.6
  3.2 0.1 broadcast_in_dim_reshape_squeeze.2
  3.3 0.2 select_reduce_fusion
  3.5 0.2 select_reduce_fusion.1
  3.7 0.6 reshape.60.pick_ref
  4.3 0.8 pad_dynamic-slice_fusion
  5.1 0.8 copy.18
  6.0 0.7 pad.5.dec_new_ref
  6.7 1.0 copy.20
  7.6 0.7 copy.17
  8.3 1.7 %copy.16 = bf16[2,256,256]{2,1,0:T(8,128)(2,1)} copy(bf16[2,256,256]{2,0,1:T(2,128)(2,1)} %bitcast.21) | data formatting | bytes 524288 | tf_op jit(solution)/shard_map/transpose | solution.py:490
  10.0 1.1 and_select_fusion.bias_ref
  11.0 121.6 %shard_map.112 = (bf16[1,256,2048]{2,1,0:T(8,128)(2,1)}, bf16[1,48,2048]{2,1,0:T(8,128)(2,1)}, bf16[4,8,2,16,256]{4,3,2,1,0:T(8,128)(2,1)}) custom-call(bf16[256,2048]{1,0:T(8,128)(2,1)} %query_ref.1, bf16[2,16,16,256]{3,2,1,0:T(8,128)(2,1)} %bitcast.16, f32[256,768]{1,0:T(8,128)} %and_select_fusion.bias_ref, bf16[24,32,128]{2,1,0:T(8,128)(2,1)} %bitcast.18, ...), custom_call_target="tpu_custom_call" | custom-call | tf_op jit(solution)/shard_map/pallas_call | solution.py:423
  132.7 2.4 %copy.19 = bf16[1,4,8,16,2,256]{5,4,3,2,1,0:T(2,128)(2,1)} copy(bf16[1,4,8,16,2,256]{5,3,4,2,1,0:T(8,128)(2,1)} %bitcast.20) | data formatting | bytes 1048576
  135.0 2.3 %copy.23 = bf16[256,2048]{1,0:T(8,128)(2,1)} copy(bf16[256,2048]{1,0:T(8,128)(2,1)} %bitcast.17) | data formatting | bytes 2097152
  137.3 1.6 %copy.24 = bf16[2,24,2048]{2,1,0:T(8,128)(2,1)} copy(bf16[2,24,2048]{2,1,0:T(8,128)(2,1)} %bitcast.23) | data formatting | bytes 393216
  (4 shorter events, 0.1 us)

commit v4 on v3

--- a/solution.py
+++ b/solution.py
@@ -39,6 +39,7 @@
     weight,
     outgoing,
     landed,
+    paired,
     total,
     cache,
     held,
@@ -50,6 +51,8 @@
     kv_recv,
     ring_send,
     ring_recv,
+    pair_send,
+    pair_recv,
     part_send,
     part_recv,
 ):
@@ -59,7 +62,10 @@
     me = lax.axis_index("pool")
     lane = lax.axis_index("tensor")
     columns = weight_ref.shape[1]
-    tile = min(COLUMN_TILE, columns)
+    half = columns // 2
+    tile = min(COLUMN_TILE, half)
+    core = lane % 2
+    partner = lane - core + (1 - core)
     has_left = me > 0
     has_right = me < pool - 1
 
@@ -117,25 +123,36 @@
             device_id_type=MESH,
         )
 
-    def part_copy(member, chunk):
-        start, size = chunks[chunk]
-        target = member // slot_members
-        return pltpu.make_async_remote_copy(
-            src_ref=outgoing.at[member, pl.ds(start, size)],
-            dst_ref=landed.at[lane, member % slot_members, pl.ds(start, size)],
-            send_sem=part_send.at[member, chunk],
-            recv_sem=part_recv.at[lane, member % slot_members, chunk],
-            device_id=(group, me, target),
-            device_id_type=MESH,
-        )
-
-    def arrived_copy(source, place, chunk):
+    def pair_copy(member, chunk):
         start, size = chunks[chunk]
         return pltpu.make_async_remote_copy(
-            src_ref=outgoing.at[0, pl.ds(start, size)],
-            dst_ref=landed.at[source, place, pl.ds(start, size)],
-            send_sem=part_send.at[0, chunk],
-            recv_sem=part_recv.at[source, place, chunk],
+            src_ref=outgoing.at[1 - core, member, pl.ds(start, size)],
+            dst_ref=paired.at[member, pl.ds(start, size)],
+            send_sem=pair_send.at[member, chunk],
+            recv_sem=pair_recv.at[member, chunk],
+            device_id=(group, me, partner),
+            device_id_type=MESH,
+        )
+
+    def part_copy(side, member, chunk):
+        start, size = chunks[chunk]
+        place = member % slot_members
+        return pltpu.make_async_remote_copy(
+            src_ref=outgoing.at[side, member, pl.ds(start, size)],
+            dst_ref=landed.at[lane, side, place, pl.ds(start, size)],
+            send_sem=part_send.at[side, member, chunk],
+            recv_sem=part_recv.at[lane, side, place, chunk],
+            device_id=(group, me, member // slot_members),
+            device_id_type=MESH,
+        )
+
+    def arrived_copy(source, side, place, chunk):
+        start, size = chunks[chunk]
+        return pltpu.make_async_remote_copy(
+            src_ref=outgoing.at[side, 0, pl.ds(start, size)],
+            dst_ref=landed.at[source, side, place, pl.ds(start, size)],
+            send_sem=part_send.at[side, 0, chunk],
+            recv_sem=part_recv.at[source, side, place, chunk],
             device_id=(group, me, source),
             device_id_type=MESH,
         )
@@ -159,11 +176,27 @@
 
             @pl.when(jnp.logical_not(mine))
             def _():
-                outgoing[member, pl.ds(start, size), place] = part.astype(jnp.bfloat16)
-
-        @pl.when(jnp.logical_not(mine))
+                outgoing[
+                    index * tile // half,
+                    member,
+                    pl.ds(start, size),
+                    pl.ds(pl.multiple_of(index * tile % half, tile), tile),
+                ] = part.astype(jnp.bfloat16)
+
+        @pl.when(member // slot_members == partner)
         def _():
-            part_copy(member, chunk).start()
+            part_copy(0, member, chunk).start()
+            part_copy(1, member, chunk).start()
+
+        @pl.when(member // slot_members // 2 != lane // 2)
+        def _():
+            pair_copy(member, chunk).start()
+            pair_copy(member, chunk).wait_recv()
+            outgoing[core, member, pl.ds(start, size), :] = (
+                outgoing[core, member, pl.ds(start, size), :].astype(jnp.float32)
+                + paired[member, pl.ds(start, size), :].astype(jnp.float32)
+            ).astype(jnp.bfloat16)
+            part_copy(core, member, chunk).start()
 
     def kv_copy(member, way):
         block = held.at[back + member]
@@ -363,18 +396,26 @@
     for place in range(slot_members):
         for chunk in range(len(chunks)):
             start, size = chunks[chunk]
-            for step in range(1, tensor):
-                arrived_copy(lax.rem(lane + step, tensor), place, chunk).wait_recv()
+            for side in range(2):
+                arrived_copy(partner, side, place, chunk).wait_recv()
+                for step in range(1, tensor // 2):
+                    chip = lax.rem(lane // 2 + step, tensor // 2)
+                    arrived_copy(2 * chip + side, side, place, chunk).wait_recv()
 
             @pl.loop(0, columns // tile)
             def _(index):
                 span = pl.ds(pl.multiple_of(index * tile, tile), tile)
                 value = total[place, pl.ds(start, size), span]
-                for step in range(1, tensor):
-                    source = lax.rem(lane + step, tensor)
-                    value = value + landed[source, place, pl.ds(start, size), span].astype(
-                        jnp.float32
-                    )
+                side = index * tile // half
+                inside = pl.ds(pl.multiple_of(index * tile % half, tile), tile)
+                value = value + landed[partner, side, place, pl.ds(start, size), inside].astype(
+                    jnp.float32
+                )
+                for step in range(1, tensor // 2):
+                    chip = lax.rem(lane // 2 + step, tensor // 2)
+                    value = value + landed[
+                        2 * chip + side, side, place, pl.ds(start, size), inside
+                    ].astype(jnp.float32)
                 if chunk == dec_chunk:
                     dec_ref[place, :, span] = value.astype(jnp.bfloat16)
                 else:
@@ -397,9 +438,15 @@
                     kv_copy(member, 1).wait_send()
                 ring_copy(member, chunk, 1).wait_send()
 
-            @pl.when(member // slot_members != lane)
-            def _():
-                part_copy(member, chunk).wait_send()
+            @pl.when(member // slot_members == partner)
+            def _():
+                part_copy(0, member, chunk).wait_send()
+                part_copy(1, member, chunk).wait_send()
+
+            @pl.when(member // slot_members // 2 != lane // 2)
+            def _():
+                pair_copy(member, chunk).wait_send()
+                part_copy(core, member, chunk).wait_send()
 
 
 def attend_and_project(
@@ -432,8 +479,9 @@
         scratch_shapes=[
             pltpu.VMEM((pool, rows, depth), jnp.bfloat16),
             pltpu.VMEM((depth, columns), jnp.bfloat16),
-            pltpu.VMEM((pool, rows, columns), jnp.bfloat16),
-            pltpu.VMEM((tensor, slot_members, rows, columns), jnp.bfloat16),
+            pltpu.VMEM((2, pool, rows, columns // 2), jnp.bfloat16),
+            pltpu.VMEM((tensor, 2, slot_members, rows, columns // 2), jnp.bfloat16),
+            pltpu.VMEM((pool, rows, columns // 2), jnp.bfloat16),
             pltpu.VMEM((slot_members, rows, columns), jnp.float32),
             pltpu.VMEM(dec_cache.shape, jnp.bfloat16),
             pltpu.VMEM((back + pool,) + kv_blocks.shape, jnp.bfloat16),
@@ -446,7 +494,9 @@
             pltpu.SemaphoreType.DMA((2, pool, count)),
             pltpu.SemaphoreType.DMA((pool, count)),
             pltpu.SemaphoreType.DMA((pool, count)),
-            pltpu.SemaphoreType.DMA((tensor, slot_members, count)),
+            pltpu.SemaphoreType.DMA((pool, count)),
+            pltpu.SemaphoreType.DMA((2, pool, count)),
+            pltpu.SemaphoreType.DMA((tensor, 2, slot_members, count)),
         ],
         compiler_params=pltpu.CompilerParams(
             collective_id=0, has_side_effects=True, vmem_limit_bytes=58 * 1024 * 1024

time: 139 us -> 136 us (0.978)
  Pallas kernels: 122 us -> 117 us
    pallas_call x1, Pallas kernels: 122 us -> 117 us  [attend_and_project(): pl.pallas_call(functools.partial(layer_kernel, chunks, slot_members, scal...]
where the time goes in v4:
time: 136 us; the launch traced here: 135 us
  Pallas kernels  117 us (86%)
  local copies, waits for them, and re-layouts  13.1 us (10%)
  other arithmetic  3.53 us (3%)
    pallas_call x1, Pallas kernels, attend_and_project(): pl.pallas_call(functools.partial(layer_kernel, chunks, slot_members, scal...  117 us
    unnamed x5, local copies, waits for them, and re-layouts  7.74 us

profile of v4, /device:TPU:0, one launch (start us, length us, event | category | flops | bytes accessed | tf_op | source)
XLA Modules:
  0.0 134.8 jit_solution(9709432694911836064)
XLA Ops:
  0.6 0.5 broadcast.28
  1.1 1.3 reduce.3
  2.5 0.8 dynamic_slice.6
  3.2 0.1 broadcast_in_dim_reshape_squeeze.2
  3.3 0.2 select_reduce_fusion
  3.5 0.2 select_reduce_fusion.1
  3.7 0.6 reshape.60.pick_ref
  4.3 0.8 pad_dynamic-slice_fusion
  5.1 0.8 copy.18
  6.0 0.7 pad.5.dec_new_ref
  6.7 1.0 copy.20
  7.6 0.7 copy.17
  8.3 1.7 %copy.16 = bf16[2,256,256]{2,1,0:T(8,128)(2,1)} copy(bf16[2,256,256]{2,0,1:T(2,128)(2,1)} %bitcast.21) | data formatting | bytes 524288 | tf_op jit(solution)/shard_map/transpose | solution.py:540
  10.0 1.1 and_select_fusion.bias_ref
  11.0 117.5 %shard_map.112 = (bf16[1,256,2048]{2,1,0:T(8,128)(2,1)}, bf16[1,48,2048]{2,1,0:T(8,128)(2,1)}, bf16[4,8,2,16,256]{4,3,2,1,0:T(8,128)(2,1)}) custom-call(bf16[256,2048]{1,0:T(8,128)(2,1)} %query_ref.1, bf16[2,16,16,256]{3,2,1,0:T(8,128)(2,1)} %bitcast.16, f32[256,768]{1,0:T(8,128)} %and_select_fusion.bias_ref, bf16[24,32,128]{2,1,0:T(8,128)(2,1)} %bitcast.18, ...), custom_call_target="tpu_custom_call" | custom-call | tf_op jit(solution)/shard_map/pallas_call | solution.py:470
  128.5 2.4 %copy.19 = bf16[1,4,8,16,2,256]{5,4,3,2,1,0:T(2,128)(2,1)} copy(bf16[1,4,8,16,2,256]{5,3,4,2,1,0:T(8,128)(2,1)} %bitcast.20) | data formatting | bytes 1048576
  130.9 2.3 %copy.23 = bf16[256,2048]{1,0:T(8,128)(2,1)} copy(bf16[256,2048]{1,0:T(8,128)(2,1)} %bitcast.17) | data formatting | bytes 2097152
  133.2 1.6 %copy.24 = bf16[2,24,2048]{2,1,0:T(8,128)(2,1)} copy(bf16[2,24,2048]{2,1,0:T(8,128)(2,1)} %bitcast.23) | data formatting | bytes 393216
  (4 shorter events, 0.1 us)
